TPU v7x, 32 devices: a whole 2x2x4 slice. The times are simulated.
32 devices in a mesh: dp: 8 (over z, y), seq: 4 (over x, core).
Axes of the slice: x: 2, y: 2, z: 4, core: 2. Of those that a mesh axis runs over, the one named last changes fastest.
Arguments:
- frames: bfloat16 [16384, 1024], P(('dp', 'seq')), may hold values from -6 to 6
- cotangent: bfloat16 [16384, 1024], P(('dp', 'seq')), may hold values from -6 to 6
- clip_len: int32 [8, 3], P('dp'), may hold values from 128 to 1792, as said below
- ln1_gain: float32 [1024], replicated, may hold values from 0.5 to 1.5
- ln1_bias: float32 [1024], replicated, may hold values from -1.75 to 1.75
- w_qkv: bfloat16 [1024, 3072], replicated, may hold values from -0.1875 to 0.1875
- w_out: bfloat16 [1024, 1024], replicated, may hold values from -0.75 to 0.75
- scale_attn: float32 [1024], replicated, may hold values from 0.5 to 1.5
- ln2_gain: float32 [1024], replicated, may hold values from 0.5 to 1.5
- ln2_bias: float32 [1024], replicated, may hold values from -1.75 to 1.75
- w_gate_up: bfloat16 [1024, 8192], replicated, may hold values from -0.1875 to 0.1875
- w_down: bfloat16 [4096, 1024], replicated, may hold values from -0.1875 to 0.1875
- scale_mlp: float32 [1024], replicated, may hold values from 0.5 to 1.5
Outputs:
- out_frames: bfloat16 [16384, 1024], P(('dp', 'seq'))
- input_grad: float32 [16384, 1024], P(('dp', 'seq'))
- grad_ln1_gain: float32 [1024], replicated
- grad_ln1_bias: float32 [1024], replicated
- grad_w_qkv: float32 [1024, 3072], P('dp', 'seq')
- grad_w_out: float32 [1024, 1024], P('dp', 'seq')
- grad_scale_attn: float32 [1024], replicated
- grad_ln2_gain: float32 [1024], replicated
- grad_ln2_bias: float32 [1024], replicated
- grad_w_gate_up: float32 [1024, 8192], P('dp', 'seq')
- grad_w_down: float32 [4096, 1024], P('dp', 'seq')
- grad_scale_mlp: float32 [1024], replicated
Inputs may be any that keep to these rules, and one draw needn't show every extreme that they name: `clip_len`: each group's clips, followed by padding of at most 32 frames, fill its 2048 frames; one clip of each group begins within the group's first 512 frames and ends within its last 512 frames.
All inputs are finite; a program needn't handle non-finite values.
Results may differ from a plain program's by a relative error of at most 0.015.
Values may be sent and summed in bfloat16 or wider, within the bound.
A program may use at most 256 MiB of HBM per device.

v0:
```python
import jax
import jax.numpy as jnp
from jax import lax
from jax.sharding import PartitionSpec as P

D = 1024
HEADS = 16
HEAD_DIM = 64
FF = 4096
HALF = 64
QBLK = 512


EPS = 1e-05
NEG = -1e30


def layer_norm(values, ln_gain, ln_bias):
    average = jnp.mean(values, -1, keepdims=True)
    centered = values - average
    variance = jnp.mean(centered * centered, -1, keepdims=True)
    return centered * lax.rsqrt(variance + EPS) * ln_gain + ln_bias


def rotate(values, positions):
    half_dim = values.shape[-1] // 2
    inv_freq = 10000.0 ** (-jnp.arange(half_dim, dtype=jnp.float32) / half_dim)
    angles = positions.astype(jnp.float32)[:, None] * inv_freq[None, :]
    cosine = jnp.cos(angles)[:, None, :]
    sine = jnp.sin(angles)[:, None, :]
    first = values[..., :half_dim]
    second = values[..., half_dim:]
    return jnp.concatenate([first * cosine - second * sine, second * cosine + first * sine], -1)


def segment_ids(lengths, positions, group_len):
    clip_ends = jnp.cumsum(lengths)
    number_ids = jnp.sum((positions[:, None] >= clip_ends[None, :]).astype(jnp.int32), axis=1)
    inside = (positions >= 0) & (positions < group_len)
    return jnp.where(inside, number_ids, -1)


def window_mask(query_ids, key_ids):
    offsets = jnp.arange(key_ids.shape[0])[None, :] - jnp.arange(query_ids.shape[0])[:, None]
    return (query_ids[:, None] == key_ids[None, :]) & (offsets >= 0) & (offsets < 2 * HALF)


def gating(gate_up):
    return jax.nn.silu(gate_up[:, :FF]) * gate_up[:, FF:]


def contract_rows(left, right):
    return lax.dot_general(
        left, right, (((0,), (0,)), ((), ())), preferred_element_type=jnp.float32
    )


def contract_back(grads, weight):
    return lax.dot_general(
        grads, weight, (((1,), (1,)), ((), ())), preferred_element_type=jnp.float32
    )


def block_scores(queries, keys, query_ids, key_ids, start):
    extent = QBLK + 2 * HALF
    q_block = lax.dynamic_slice_in_dim(queries, start, QBLK, 0)
    k_block = lax.dynamic_slice_in_dim(keys, start, extent, 0)
    allowed = window_mask(
        lax.dynamic_slice_in_dim(query_ids, start, QBLK, 0),
        lax.dynamic_slice_in_dim(key_ids, start, extent, 0),
    )
    scores = jnp.einsum(
        "qhd,khd->hqk", q_block, k_block, preferred_element_type=jnp.float32
    ) * HEAD_DIM ** (-0.5)
    return (jnp.where(allowed[None], scores, NEG), q_block, k_block)


def attention_forward(queries, keys, values, query_ids, key_ids):

    def one_block(index):
        start = index * QBLK
        scores, q_block, k_block = block_scores(queries, keys, query_ids, key_ids, start)
        v_block = lax.dynamic_slice_in_dim(values, start, QBLK + 2 * HALF, 0)
        peaks = jnp.max(scores, -1, keepdims=True)
        exponent = jnp.exp(scores - peaks)
        totals = jnp.sum(exponent, -1, keepdims=True)
        probs = (exponent / totals).astype(jnp.bfloat16)
        attended = jnp.einsum("hqk,khd->qhd", probs, v_block, preferred_element_type=jnp.float32)
        return (attended, peaks, totals)

    attended, peaks, totals = lax.map(
        one_block, jnp.arange(queries.shape[0] // QBLK, dtype=jnp.int32)
    )
    return (attended.reshape(queries.shape[0], queries.shape[1], queries.shape[2]), peaks, totals)


def attention_backward(queries, keys, values, out_grads, query_ids, key_ids, peaks, totals):
    extent = QBLK + 2 * HALF
    score_scale = HEAD_DIM ** (-0.5)

    def one_block(carry, inputs):
        key_grads, value_grads = carry
        index, peak_block, total_block = inputs
        start = index * QBLK
        scores, q_block, k_block = block_scores(queries, keys, query_ids, key_ids, start)
        v_block = lax.dynamic_slice_in_dim(values, start, extent, 0)
        g_block = lax.dynamic_slice_in_dim(out_grads, start, QBLK, 0)
        probs = jnp.exp(scores - peak_block) / total_block
        value_part = jnp.einsum(
            "hqk,qhd->khd", probs.astype(jnp.bfloat16), g_block, preferred_element_type=jnp.float32
        )
        prob_grads = jnp.einsum(
            "qhd,khd->hqk", g_block, v_block, preferred_element_type=jnp.float32
        )
        inner = jnp.sum(probs * prob_grads, -1, keepdims=True)
        score_grads = (probs * (prob_grads - inner)).astype(jnp.bfloat16)
        query_part = (
            jnp.einsum("hqk,khd->qhd", score_grads, k_block, preferred_element_type=jnp.float32)
            * score_scale
        )
        key_part = (
            jnp.einsum("hqk,qhd->khd", score_grads, q_block, preferred_element_type=jnp.float32)
            * score_scale
        )
        key_grads = lax.dynamic_update_slice_in_dim(
            key_grads, lax.dynamic_slice_in_dim(key_grads, start, extent, 0) + key_part, start, 0
        )
        value_grads = lax.dynamic_update_slice_in_dim(
            value_grads,
            lax.dynamic_slice_in_dim(value_grads, start, extent, 0) + value_part,
            start,
            0,
        )
        return ((key_grads, value_grads), query_part)

    zeros_kv = jnp.zeros(keys.shape, jnp.float32)
    block_count = queries.shape[0] // QBLK
    (key_grads, value_grads), query_grads = lax.scan(
        one_block, (zeros_kv, zeros_kv), (jnp.arange(block_count, dtype=jnp.int32), peaks, totals)
    )
    return (
        query_grads.reshape(queries.shape[0], queries.shape[1], queries.shape[2]),
        key_grads,
        value_grads,
    )


def to_blocks(matrix, data_count, seq_count):
    row_total, col_total = matrix.shape
    shaped = matrix.reshape(data_count, row_total // data_count, seq_count, col_total // seq_count)
    return shaped.transpose(0, 2, 1, 3).reshape(
        data_count * seq_count, row_total // data_count, col_total // seq_count
    )


def local(
    frames,
    cotangent,
    clip_len,
    ln1_gain,
    ln1_bias,
    w_qkv,
    w_out,
    scale_attn,
    ln2_gain,
    ln2_bias,
    w_gate_up,
    w_down,
    scale_mlp,
):
    row_count = frames.shape[0]
    seq_count = lax.axis_size("seq")
    group_len = row_count * seq_count
    lengths = clip_len[0]
    own_pos = lax.axis_index("seq") * row_count + jnp.arange(row_count, dtype=jnp.int32)
    inputs32 = frames.astype(jnp.float32)
    normed, norm_back = jax.vjp(layer_norm, inputs32, ln1_gain, ln1_bias)
    normed_b = normed.astype(jnp.bfloat16)
    projected = jnp.dot(normed_b, w_qkv, preferred_element_type=jnp.float32)
    turned = rotate(projected[:, : 2 * D].reshape(row_count, 2 * HEADS, HEAD_DIM), own_pos)
    rotated = jnp.concatenate([turned.reshape(row_count, 2 * D), projected[:, 2 * D :]], 1).astype(
        jnp.bfloat16
    )
    margin = ((HALF, HALF), (0, 0), (0, 0))
    q_heads, k_heads, v_heads = (
        lax.all_to_all(rotated[:, :D], "seq", split_axis=1, concat_axis=0, tiled=True),
        lax.all_to_all(rotated[:, D : 2 * D], "seq", split_axis=1, concat_axis=0, tiled=True),
        lax.all_to_all(rotated[:, 2 * D :], "seq", split_axis=1, concat_axis=0, tiled=True),
    )
    local_heads = HEADS // seq_count
    all_pos = jnp.arange(group_len, dtype=jnp.int32)
    query_ids = segment_ids(lengths, all_pos, group_len)
    key_ids = segment_ids(lengths, jnp.arange(-HALF, group_len + HALF, dtype=jnp.int32), group_len)
    queries = q_heads.reshape(group_len, local_heads, HEAD_DIM)
    keys = jnp.pad(k_heads.reshape(group_len, local_heads, HEAD_DIM), margin)
    values = jnp.pad(v_heads.reshape(group_len, local_heads, HEAD_DIM), margin)
    attended, peaks, totals = attention_forward(queries, keys, values, query_ids, key_ids)
    attended_t = lax.all_to_all(
        attended.reshape(group_len, local_heads * HEAD_DIM).astype(jnp.bfloat16),
        "seq",
        split_axis=0,
        concat_axis=1,
        tiled=True,
    )
    branch = jnp.dot(attended_t, w_out, preferred_element_type=jnp.float32)
    middle = inputs32 + scale_attn * branch
    normed_two, norm_two_back = jax.vjp(layer_norm, middle, ln2_gain, ln2_bias)
    normed_two_b = normed_two.astype(jnp.bfloat16)
    gate_up = jnp.dot(normed_two_b, w_gate_up, preferred_element_type=jnp.float32)
    hidden, gate_back = jax.vjp(gating, gate_up)
    hidden_b = hidden.astype(jnp.bfloat16)
    mlp_out = jnp.dot(hidden_b, w_down, preferred_element_type=jnp.float32)
    out_frames = (middle + scale_mlp * mlp_out).astype(jnp.bfloat16)
    out_grad = cotangent.astype(jnp.float32)
    grad_scale_mlp = jnp.sum(out_grad * mlp_out, 0)
    mlp_grad = (out_grad * scale_mlp).astype(jnp.bfloat16)
    grad_w_down = contract_rows(hidden_b, mlp_grad)
    hidden_grad = contract_back(mlp_grad, w_down)
    (gate_up_grad,) = gate_back(hidden_grad)
    gate_up_b = gate_up_grad.astype(jnp.bfloat16)
    grad_w_gate_up = contract_rows(normed_two_b, gate_up_b)
    middle_part, grad_ln2_gain, grad_ln2_bias = norm_two_back(contract_back(gate_up_b, w_gate_up))
    middle_grad = out_grad + middle_part
    grad_scale_attn = jnp.sum(middle_grad * branch, 0)
    branch_grad = (middle_grad * scale_attn).astype(jnp.bfloat16)
    grad_w_out = contract_rows(attended_t, branch_grad)
    attended_grad = contract_back(branch_grad, w_out).astype(jnp.bfloat16)
    grad_heads = lax.all_to_all(attended_grad, "seq", split_axis=1, concat_axis=0, tiled=True)
    query_grads, key_grads, value_grads = attention_backward(
        queries,
        keys,
        values,
        grad_heads.reshape(group_len, local_heads, HEAD_DIM),
        query_ids,
        key_ids,
        peaks,
        totals,
    )
    query_back = (
        rotate(query_grads, -all_pos)
        .reshape(group_len, local_heads * HEAD_DIM)
        .astype(jnp.bfloat16)
    )
    key_back = (
        rotate(key_grads[HALF : HALF + group_len], -all_pos)
        .reshape(group_len, local_heads * HEAD_DIM)
        .astype(jnp.bfloat16)
    )
    value_back = (
        value_grads[HALF : HALF + group_len]
        .reshape(group_len, local_heads * HEAD_DIM)
        .astype(jnp.bfloat16)
    )
    query_own, key_own, value_own = (
        lax.all_to_all(query_back, "seq", split_axis=0, concat_axis=1, tiled=True),
        lax.all_to_all(key_back, "seq", split_axis=0, concat_axis=1, tiled=True),
        lax.all_to_all(value_back, "seq", split_axis=0, concat_axis=1, tiled=True),
    )
    projected_grad = jnp.concatenate([query_own, key_own, value_own], 1)
    grad_w_qkv = contract_rows(normed_b, projected_grad)
    input_part, grad_ln1_gain, grad_ln1_bias = norm_back(contract_back(projected_grad, w_qkv))
    input_grad = middle_grad + input_part
    vector_grads = jnp.stack(
        [
            grad_ln1_gain,
            grad_ln1_bias,
            grad_scale_attn,
            grad_ln2_gain,
            grad_ln2_bias,
            grad_scale_mlp,
        ],
        0,
    )
    vector_total = lax.psum(vector_grads, ("dp", "seq"))
    data_count = lax.axis_size("dp")
    summed = (
        lax.psum_scatter(
            to_blocks(grad_w_qkv, data_count, seq_count),
            ("dp", "seq"),
            scatter_dimension=0,
            tiled=True,
        ),
        lax.psum_scatter(
            to_blocks(grad_w_out, data_count, seq_count),
            ("dp", "seq"),
            scatter_dimension=0,
            tiled=True,
        ),
        lax.psum_scatter(
            to_blocks(grad_w_gate_up, data_count, seq_count),
            ("dp", "seq"),
            scatter_dimension=0,
            tiled=True,
        ),
        lax.psum_scatter(
            to_blocks(grad_w_down, data_count, seq_count),
            ("dp", "seq"),
            scatter_dimension=0,
            tiled=True,
        ),
    )
    sum_qkv = summed[0][0]
    sum_out = summed[1][0]
    sum_gate_up = summed[2][0]
    sum_down = summed[3][0]
    return (
        out_frames,
        input_grad,
        vector_total[0],
        vector_total[1],
        sum_qkv,
        sum_out,
        vector_total[2],
        vector_total[3],
        vector_total[4],
        sum_gate_up,
        sum_down,
        vector_total[5],
    )


def solution(mesh):
    return jax.shard_map(
        local,
        mesh=mesh,
        in_specs=(
            P(("dp", "seq"), None),
            P(("dp", "seq"), None),
            P("dp", None),
            P(),
            P(),
            P(),
            P(),
            P(),
            P(),
            P(),
            P(),
            P(),
            P(),
        ),
        out_specs=(
            P(("dp", "seq"), None),
            P(("dp", "seq"), None),
            P(),
            P(),
            P("dp", "seq"),
            P("dp", "seq"),
            P(),
            P(),
            P(),
            P("dp", "seq"),
            P("dp", "seq"),
            P(),
        ),
        check_vma=False,
    )
```

profile of v0, /device:TPU:0, one launch (start us, length us, event | category | flops | bytes accessed | tf_op | source)
XLA Modules:
  0.0 1286.3 jit_solution(16726535134713375335)
XLA Ops:
  11.1 5.8 fusion.83
  21.9 5.3 copy.86
  27.5 2.9 subtract_convert_fusion
  31.8 18.6 %all_to_all.128 = bf16[512,4,256]{0,2,1:T(8,128)(2,1)} all-to-all(bf16[512,4,256]{0,2,1:T(8,128)(2,1)S(1)} %bitcast.169), channel_id=1, replica_groups=mesh['dp'=8,'seq'=4] {'seq'}, dimensions={1} | all-to-all | bytes 2097152 | tf_op jit(solution)/shard_map/all_to_all | solution.py:186
  50.4 3.6 all-to-all-start.2
  59.3 9.2 all-to-all-done.2
  68.5 4.4 all-to-all-start
  73.2 3.0 copy.87
  83.2 4.2 all-to-all-done
  93.9 36.7 %while.28 = (s32[]{:T(128)}, bf16[4,512,4,64]{1,3,2,0:T(8,128)(2,1)}, f32[4,4,512,1]{2,1,3,0:T(4,128)}, f32[4,4,512,1]{2,1,3,0:T(4,128)S(1)}, s32[4]{0:T(128)S(1...) while((s32[]{:T(128)}, ...), condition=%wide.region_8.9_spmd, body=%wide.region_5.8_spmd.sunk | while | flops 353234944 | bytes 26957628 | solution.py:91
  99.2 2.8 fusion.130
  108.4 2.8 fusion.130
  117.6 2.8 fusion.130
  126.7 2.8 fusion.130
  130.6 18.4 %all_to_all.129 = bf16[4,512,256]{1,2,0:T(8,128)(2,1)S(1)} all-to-all(bf16[4,512,256]{1,2,0:T(8,128)(2,1)} %bitcast.173), channel_id=1, replica_groups=mesh['dp'=8,'seq'=4] {'seq'}, dimensions={0} | all-to-all | bytes 2097152 | tf_op jit(solution)/shard_map/all_to_all | solution.py:198
  153.0 15.9 %fusion.86 = f32[512,8192]{1,0:T(8,128)} fusion(bf16[1024,8192]{1,0:T(8,128)(2,1)} %param.27, f32[512,1024]{1,0:T(8,128)S(1)} %get-tuple-element.212, f32[1024]{0:T(1024)S(1)} %copy-done.22, f32[1024]{0:T(1024)S(1)} %copy-done.20, f32[512]{0:T(512)S(1)} %fusion.77, f32[512]{0:T(512)S(1)} %broadcast_multiply_fusion), kind=kOutput, calls=%fused_computation.146 | convolution fusion | flops 8592556032 | bytes 35663872 | tf_op jit(solution)/shard_map/dot_general | solution.py:209
  168.9 17.4 %fusion.69 = (f32[512,4096]{1,0:T(8,128)}, f32[512,4096]{1,0:T(8,128)}, bf16[512,4096]{1,0:T(8,128)(2,1)}) fusion(f32[512,8192]{1,0:T(8,128)} %fusion.86, bf16[4096,1024]{1,0:T(8,128)(2,1)} %param.28, bf16[512,1024]{1,0:T(8,128)(2,1)} %param.18, f32[1024]{0:T(1024)S(1)} %copy-done.44), kind=kOutput, calls=%fused_computation.112 | convolution fusion | flops 4325900288 | bytes 47190016 | tf_op jit(solution)/shard_map/dot_general | solution.py:59
  186.3 32.7 %multiply_reduce_fusion.1 = (f32[1024]{0:T(1024)}, f32[512]{0:T(512)S(1)}, f32[1024]{0:T(1024)}, f32[512,1024]{1,0:T(8,128)}) fusion(f32[512,1024]{1,0:T(8,128)} %copy-done.2, f32[512]{0:T(512)S(1)} %fusion.77, f32[512]{0:T(512)S(1)} %broadcast_multiply_fusion, f32[1024]{0:T(1024)S(1)} %copy-done.20, bf16[1024,8192]{1,0:T(8,128)(2,1)} %param.27, ...), kind=kOutput, calls=%fused_computation.89 | convolution fusion | flops 8602514432 | bytes 37767168 | tf_op jit(solution)/shard_map/dot_general | solution.py:59
  219.0 3.0 fusion.88
  224.4 3.5 all-to-all-start.4
  229.7 12.6 all-to-all-done.4
  248.0 100.8 %while.29 = (s32[]{:T(128)}, f32[2176,4,64]{0,2,1:T(8,128)}, f32[2176,4,64]{0,2,1:T(8,128)}, f32[4,512,4,64]{1,0,3,2:T(4,128)}, s32[4]{0:T(128)S(1)}, /*index=5*...) while((s32[]{:T(128)}, f32[2176,4,64]{0,2,1:T(8,128)}, ...), condition=%wide.region_15.16_spmd, body=%wide.region_13.15_spmd.sunk | while | flops 854554624 | bytes 47331124 | solution.py:138
  262.1 11.1 dynamic_update_slice.34
  287.2 11.1 dynamic_update_slice.34
  312.5 11.1 dynamic_update_slice.34
  337.7 11.1 dynamic_update_slice.34
  348.8 2.7 reshape.426
  356.2 3.5 all-to-all-start.5
  361.7 12.5 all-to-all-done.5
  374.1 4.2 all-to-all-start.6
  381.9 11.0 all-to-all-done.6
  392.9 16.9 %all_to_all.130 = bf16[4,512,256]{1,2,0:T(8,128)(2,1)S(1)} all-to-all(bf16[4,512,256]{1,2,0:T(8,128)(2,1)S(1)} %copy.94), channel_id=1, replica_groups=mesh['dp'=8,'seq'=4] {'seq'}, dimensions={0} | all-to-all | bytes 2097152 | tf_op jit(solution)/shard_map/all_to_all | solution.py:257
  409.9 7.4 fusion.87
  419.1 9.6 fusion.64
  431.0 4.8 fusion.92
  436.5 10.2 fusion.65
  446.7 15.9 %reshape.431 = f32[8,128,4,768]{3,2,1,0:T(4,128)} reshape(f32[1024,3072]{1,0:T(8,128)} %fusion.65) | data formatting | bytes 25165824 | tf_op jit(solution)/shard_map/reshape | solution.py:150
  462.6 11.3 copy.95
  475.1 10.4 fusion.70
  485.5 20.4 %reshape.436 = f32[8,512,4,256]{3,2,1,0:T(4,128)} reshape(f32[4096,1024]{1,0:T(8,128)} %fusion.70) | data formatting | bytes 33554432 | tf_op jit(solution)/shard_map/reshape | solution.py:150
  505.9 14.2 %copy.98 = f32[8,4,512,256]{3,2,1,0:T(8,128)} copy(f32[8,4,512,256]{3,1,2,0:T(4,128)} %bitcast.155) | data formatting | bytes 33554432 | tf_op jit(solution)/shard_map/transpose | solution.py:151
  520.8 20.8 %fusion.67 = f32[1024,8192]{1,0:T(8,128)} fusion(f32[512,4096]{1,0:T(8,128)} %get-tuple-element.222, f32[512,4096]{1,0:T(8,128)} %get-tuple-element.221, f32[512,1024]{1,0:T(8,128)S(1)} %copy-done.3, f32[1024]{0:T(1024)S(1)} %copy-done.23, f32[1024]{0:T(1024)S(1)} %copy-done.21, f32[512]{0:T(512)S(1)} %copy-done.27, f32[512]{0:T(512)S(1)} %copy-done.25), kind=kOutput, calls=%fused_computation.102 | convolution fusion | flops 8600944640 | bytes 52441088 | tf_op jit(solution)/shard_map/dot_general | solution.py:53
  541.6 39.6 %reshape.434 = f32[8,128,4,2048]{3,2,1,0:T(4,128)} reshape(f32[1024,8192]{1,0:T(8,128)} %fusion.67) | data formatting | bytes 67108864 | tf_op jit(solution)/shard_map/reshape | solution.py:150
  581.2 32.6 %copy.97 = f32[8,4,128,2048]{3,2,1,0:T(8,128)} copy(f32[8,4,128,2048]{3,1,2,0:T(4,128)} %bitcast.153) | data formatting | bytes 67108864 | tf_op jit(solution)/shard_map/transpose | solution.py:151
  614.5 41.3 %psum.7 = f32[6,1024]{1,0:T(8,128)S(1)} all-reduce(f32[6,1024]{1,0:T(8,128)S(1)} %stack.15), channel_id=1, replica_groups=mesh['dp'=8,'seq'=4] {'dp','seq'}, use_global_device_ids=true, to_apply=%region_24.25 | all-reduce | flops 6144 | bytes 49152 | tf_op jit(solution)/shard_map/psum | solution.py:274
  656.5 79.4 %reduce-scatter.5.cloned.1.call-done = f32[1,128,768]{2,1,0:T(8,128)} async-done(((f32[32,128,768]{2,1,0:T(8,128)}), f32[1,128,768]{2,1,0:T(8,128)}) %reduce-scatter.5.cloned.1.call-update) | async-done | bytes 393232 | tf_op jit(solution)/shard_map/reduce_scatter | solution.py:277
  735.8 185.1 %reduce-scatter.11.cloned.1.call-done = f32[1,512,256]{2,1,0:T(8,128)} async-done(((f32[32,512,256]{2,1,0:T(8,128)}), f32[1,512,256]{2,1,0:T(8,128)}) %reduce-scatter.11.cloned.1.call-update) | async-done | bytes 524304 | tf_op jit(solution)/shard_map/reduce_scatter | solution.py:295
  920.9 358.7 %reduce-scatter.9.cloned.1.call-done = f32[1,128,2048]{2,1,0:T(8,128)} async-done(((f32[32,128,2048]{2,1,0:T(8,128)}), f32[1,128,2048]{2,1,0:T(8,128)}) %reduce-scatter.9.cloned.1.call-update) | async-done | bytes 1048592 | tf_op jit(solution)/shard_map/reduce_scatter | solution.py:289
  (254 shorter events, 137.4 us)
Async XLA Ops:
  7.2 141.8 %copy-start = (bf16[1024,1024]{1,0:T(8,128)(2,1)S(1)}, bf16[1024,1024]{1,0:T(8,128)(2,1)}, u32[]{:S(2)}) copy-start(bf16[1024,1024]{1,0:T(8,128)(2,1)} %param.23) | copy-start | bytes 6291460
  7.2 3.9 copy-start.4
  7.2 3.9 copy-start.35
  7.2 3.9 copy-start.42
  8.9 8.0 copy-start.28
  11.1 5.8 copy-start.33
  16.9 2.7 copy-start.9
  50.4 6.4 copy-start.45
  50.4 18.1 %all-to-all-start.2 = ((bf16[512,4,256]{0,2,1:T(8,128)(2,1)}), bf16[512,4,256]{0,2,1:T(8,128)(2,1)S(1)}, u32[]{:S(2)}, u32[]{:S(2)}) async-start(bf16[512,4,256]{0,2,1:T(8,128)(2,1)} %bitcast.168), calls=%async_computation.2 | async-start | bytes 2097152 | tf_op jit(solution)/shard_map/all_to_all | solution.py:187
  68.5 19.0 %all-to-all-start = ((bf16[512,4,256]{2,0,1:T(8,128)(2,1)}), bf16[512,4,256]{2,0,1:T(8,128)(2,1)}, u32[]{:S(2)}, u32[]{:S(2)}) async-start(bf16[512,4,256]{2,0,1:T(8,128)(2,1)} %bitcast.165), calls=%async_computation | async-start | bytes 2097152 | tf_op jit(solution)/shard_map/all_to_all | solution.py:188
  91.9 1.5 copy-start.10
  97.8 1.5 copy-start.16
  106.9 1.5 copy-start.16
  116.1 1.5 copy-start.16
  125.3 1.5 copy-start.16
  130.6 18.4 %copy-start.5 = (bf16[512,1024]{1,0:T(8,128)(2,1)S(1)}, bf16[512,1024]{1,0:T(8,128)(2,1)}, u32[]{:S(2)}) copy-start(bf16[512,1024]{1,0:T(8,128)(2,1)} %param.17) | copy-start | bytes 3145732
  130.6 18.4 %copy-start.32 = (f32[1024]{0:T(1024)S(1)}, f32[1024]{0:T(1024)}, u32[]{:S(2)}) copy-start(f32[1024]{0:T(1024)} %param.24) | copy-start | bytes 12292
  149.0 2.7 copy-start.8
  151.6 1.3 copy-start.22
  151.6 67.3 %copy-start.24 = (f32[512]{0:T(512)}, f32[512]{0:T(512)S(1)}, u32[]{:S(2)}) copy-start(f32[512]{0:T(512)S(1)} %broadcast_multiply_fusion) | copy-start | bytes 6148
  153.0 66.0 %copy-start.26 = (f32[512]{0:T(512)}, f32[512]{0:T(512)S(1)}, u32[]{:S(2)}) copy-start(f32[512]{0:T(512)S(1)} %fusion.77) | copy-start | bytes 6148
  153.0 15.9 %copy-start.44 = (f32[1024]{0:T(1024)S(1)}, f32[1024]{0:T(1024)}, u32[]{:S(2)}) copy-start(f32[1024]{0:T(1024)} %param.29) | copy-start | bytes 12292
  219.0 3.0 copy-start.39
  222.0 1.4 copy-start.11
  224.4 18.0 %all-to-all-start.4 = ((bf16[512,4,256]{2,0,1:T(8,128)(2,1)}), bf16[512,4,256]{2,0,1:T(8,128)(2,1)S(1)}, u32[]{:S(2)}, u32[]{:S(2)}) async-start(bf16[512,4,256]{2,0,1:T(8,128)(2,1)} %bitcast.130), calls=%async_computation.4 | async-start | bytes 2097152 | tf_op jit(solution)/shard_map/all_to_all | solution.py:228
  245.0 3.0 copy-start.7
  348.8 2.7 copy-start.19
  356.2 18.0 %all-to-all-start.5 = ((bf16[4,512,256]{1,2,0:T(8,128)(2,1)}), bf16[4,512,256]{1,2,0:T(8,128)(2,1)S(1)}, u32[]{:S(2)}, u32[]{:S(2)}) async-start(bf16[4,512,256]{1,2,0:T(8,128)(2,1)} %copy.92), calls=%async_computation.5 | async-start | bytes 2097152 | tf_op jit(solution)/shard_map/all_to_all | solution.py:255
  374.1 6.3 copy-start.14
  374.1 18.8 %all-to-all-start.6 = ((bf16[4,512,256]{1,2,0:T(8,128)(2,1)}), bf16[4,512,256]{1,2,0:T(8,128)(2,1)}, u32[]{:S(2)}, u32[]{:S(2)}) async-start(bf16[4,512,256]{1,2,0:T(8,128)(2,1)} %copy.93), calls=%async_computation.6 | async-start | bytes 2097152 | tf_op jit(solution)/shard_map/all_to_all | solution.py:256
  378.4 278.1 %reduce-scatter.7.cloned.1.call-start = ((), (), s32[]{:S(2)}) async-start(), calls=%async_computation.13 | async-start | bytes 4325376 | tf_op jit(solution)/shard_map/reduce_scatter | solution.py:283
  381.6 28.1 %copy-start.6 = (bf16[512,1024]{1,0:T(8,128)(2,1)S(1)}, bf16[512,1024]{1,0:T(8,128)(2,1)}, u32[]{:S(2)}) copy-start(bf16[512,1024]{1,0:T(8,128)(2,1)} %param.17) | copy-start | bytes 3145732
  381.6 28.1 %copy-start.29 = (f32[512]{0:T(512)S(1)}, f32[512]{0:T(512)}, u32[]{:S(2)}) copy-start(f32[512]{0:T(512)} %copy-done.28) | copy-start | bytes 6148
  381.7 28.1 %copy-start.36 = (f32[1024]{0:T(1024)S(1)}, f32[1024]{0:T(1024)}, u32[]{:S(2)}) copy-start(f32[1024]{0:T(1024)} %param.20) | copy-start | bytes 12292
  381.9 27.9 %copy-start.15 = (bf16[4,512,256]{1,2,0:T(8,128)(2,1)S(1)}, bf16[4,512,256]{1,2,0:T(8,128)(2,1)}, u32[]{:S(2)}) copy-start(bf16[4,512,256]{1,2,0:T(8,128)(2,1)} %copy-done.14) | copy-start | bytes 3145732
  409.8 7.5 copy-start.18
  409.8 8.6 slice-start
  409.8 7.5 copy-start.31
  409.8 7.5 copy-start.34
  409.8 8.5 copy-start.12
  409.8 8.5 copy-start.13
  409.8 8.5 slice-start.1
  417.3 1.6 copy-start.3
  417.3 1.8 copy-start.40
  435.8 300.0 %reduce-scatter.5.cloned.1.call-start = ((), (), s32[]{:S(2)}) async-start(), calls=%async_computation.12 | async-start | bytes 12976128 | tf_op jit(solution)/shard_map/reduce_scatter | solution.py:277
  473.9 447.0 %reduce-scatter.11.cloned.1.call-start = ((), (), s32[]{:S(2)}) async-start(), calls=%async_computation.15 | async-start | bytes 17301504 | tf_op jit(solution)/shard_map/reduce_scatter | solution.py:295
  520.1 759.5 %reduce-scatter.9.cloned.1.call-start = ((), (), s32[]{:S(2)}) async-start(), calls=%async_computation.14 | async-start | bytes 34603008 | tf_op jit(solution)/shard_map/reduce_scatter | solution.py:289
  613.8 665.8 %copy-start.1 = (bf16[1024,1024]{1,0:T(8,128)(2,1)S(1)}, bf16[1024,1024]{1,0:T(8,128)(2,1)}, u32[]{:S(2)}) copy-start(bf16[1024,1024]{1,0:T(8,128)(2,1)} %param.23) | copy-start | bytes 6291460
  (15 other events, 13.3 us)
Sparse Core Ops, SparseCore 0:
  436.0 141.6 reduce-scatter.6
  584.2 151.5 reduce-scatter.4
  738.8 182.0 reduce-scatter.10
  923.7 355.8 reduce-scatter.8
where the time goes:
time: 1300 us; the launch traced here: 1290 us
  waiting for transfers between devices  673 us (52%)
  local copies, waits for them, and re-layouts  251 us (19%)
  matrix products  202 us (16%)
  blocking collectives  95.1 us (7%)
  other arithmetic  25.8 us (2%)
  starting transfers between devices  19.9 us (2%)
  between operations  14.7 us (1%)
    reduce_scatter x1, waiting for transfers between devices, local(): lax.psum_scatter(to_blocks(grad_w_gate_up, data_count, seq_count), ('dp',...  359 us
    reduce_scatter x1, waiting for transfers between devices, local(): lax.psum_scatter(to_blocks(grad_w_down, data_count, seq_count), ('dp', 's...  185 us
    reduce_scatter x1, waiting for transfers between devices, local(): lax.psum_scatter(to_blocks(grad_w_qkv, data_count, seq_count), ('dp', 'se...  79.4 us
    reshape x3, local copies, waits for them, and re-layouts, to_blocks(): matrix.reshape(data_count, row_total // data_count, seq_count, col_total...  75.9 us
    dot_general x4, matrix products, contract_back(): lax.dot_general(grads, weight, (((1,), (1,)), ((), ())), preferred_elemen...  58.8 us
    transpose x3, local copies, waits for them, and re-layouts, to_blocks(): shaped.transpose(0, 2, 1, 3)  58 us
    dynamic_update_slice x12, local copies, waits for them, and re-layouts, attention_forward(): lax.map(one_block, jnp.arange(queries.shape[0] // QBLK, dtype=jnp.int32))  49.1 us
    dot_general x4, matrix products, contract_rows(): lax.dot_general(left, right, (((0,), (0,)), ((), ())), preferred_element_...  46.2 us
  transfers between devices with their start and end apart: 9, of which 8 were waited for; matrix products, arithmetic and copies ran while one was open for 15% of the time, Pallas kernels for 0%

commit v1 on v0

--- a/solution.py
+++ b/solution.py
@@ -1,6 +1,10 @@
+import functools
+
 import jax
 import jax.numpy as jnp
 from jax import lax
+from jax.experimental import pallas as pl
+from jax.experimental.pallas import tpu as pltpu
 from jax.sharding import PartitionSpec as P
 
 D = 1024
@@ -151,6 +155,414 @@
     return shaped.transpose(0, 2, 1, 3).reshape(
         data_count * seq_count, row_total // data_count, col_total // seq_count
     )
+
+
+MESH = pl.DeviceIdType.MESH
+TOK = 512
+PARTS = (0, 48, 96, 128)
+
+UNITS = (
+    [(2, 0, 128, 2, 2048, 256 * v, 2, 0) for v in range(8)]
+    + [(3, 128 * v, 512, 3, 256, 0, 3, 128 * v) for v in range(4)]
+    + [(1, 0, 128, 1, 256, 0, 1, 0)]
+    + [(0, 0, 128, 0, 768, 256 * v, 0, 0) for v in range(3)]
+)
+LAG = 1
+
+
+def tn_dot(left, right):
+    return lax.dot_general(
+        left, right, (((0,), (0,)), ((), ())), preferred_element_type=jnp.float32
+    )
+
+
+def scatter_kernel(
+    left0, left1, left2, left3, right0, right1, right2, right3, vec_ref,
+    out0, out1, out2, out3, vec_out,
+    far_left0, far_left1, far_left2, far_left3, far_right,
+    xbuf, ybuf, part_a, part_b, part_c,
+    recv_a1, recv_a2, recv_az, recv_b1, recv_b2, recv_bz, recv_cz, recv_c1, recv_c2,
+    vec_sum, vec_recv, vec_z,
+    far_send, far_recv, load_sem, send_sem, recv_sem, vec_send, vec_rsem,
+):
+    lefts = (left0, left1, left2, left3)
+    rights = (right0, right1, right2, right3)
+    outs = (out0, out1, out2, out3)
+    far_lefts = (far_left0, far_left1, far_left2, far_left3)
+    dp = lax.axis_index("dp")
+    seq = lax.axis_index("seq")
+    z, y = dp // 2, dp % 2
+    x, c = seq // 2, seq % 2
+    dev_c = (dp, x * 2 + 1 - c)
+    dev_x = (dp, (1 - x) * 2 + c)
+    dev_y = (z * 2 + 1 - y, seq)
+    dev_z = [(lax.rem(z + k, 4) * 2 + y, seq) for k in (1, 2, 3)]
+    count = len(UNITS)
+
+    barrier = pltpu.get_barrier_semaphore()
+    for device in [dev_c, dev_x, dev_y] + dev_z:
+        pl.semaphore_signal(barrier, inc=1, device_id=device, device_id_type=MESH)
+    pl.semaphore_wait(barrier, 6)
+
+    def remote(src, dst, ssem, rsem, device):
+        return pltpu.make_async_remote_copy(
+            src_ref=src, dst_ref=dst, send_sem=ssem, recv_sem=rsem,
+            device_id=device, device_id_type=MESH,
+        )
+
+    sends = []
+
+    def block_columns(unit, block):
+        _, _, _, right, width, offset, _, _ = UNITS[unit]
+        start = pl.multiple_of(block * width + offset, 128)
+        return rights[right].at[:, pl.ds(start, 256)]
+
+    left_copy = {}
+    right_copies = []
+    for unit in range(count):
+        left = UNITS[unit][0]
+        if left not in left_copy:
+            copy = remote(
+                lefts[left], far_lefts[left], far_send.at[left], far_recv.at[left], dev_c
+            )
+            copy.start()
+            left_copy[left] = copy
+            sends.append(copy)
+        pair = []
+        for other_x in range(2):
+            slot = 4 + 2 * unit + other_x
+            copy = remote(
+                block_columns(unit, 2 * other_x + 1 - c), far_right.at[unit, other_x],
+                far_send.at[slot], far_recv.at[slot], dev_c,
+            )
+            copy.start()
+            pair.append(copy)
+            sends.append(copy)
+        right_copies.append(pair)
+
+    left_key = [(u[0], u[1]) for u in UNITS]
+    left_slot = []
+    for unit in range(count):
+        if unit and left_key[unit] == left_key[unit - 1]:
+            left_slot.append(left_slot[-1])
+        else:
+            left_slot.append(1 - left_slot[-1] if unit else 0)
+
+    waited_left = set()
+
+    def load(unit):
+        left, offset, width, _, _, _, _, _ = UNITS[unit]
+        started = []
+        if unit == 0 or left_key[unit] != left_key[unit - 1]:
+            if left not in waited_left:
+                left_copy[left].wait_recv()
+                waited_left.add(left)
+            slot = left_slot[unit]
+            for side, array in enumerate((lefts[left], far_lefts[left])):
+                sem = load_sem.at[slot, side]
+                if width == 128:
+                    copy = pltpu.make_async_copy(array, xbuf.at[slot, side], sem)
+                    copy.start()
+                    started.append(copy)
+                else:
+                    for block in range(8):
+                        pltpu.make_async_copy(
+                            array.at[:, pl.ds(block * width + offset, 128)],
+                            xbuf.at[slot, side, :, pl.ds(block * 128, 128)],
+                            sem,
+                        ).start()
+                    started.append(
+                        pltpu.make_async_copy(
+                            array.at[:, pl.ds(0, 1024)], xbuf.at[slot, side], sem
+                        )
+                    )
+        slot = unit % 2
+        for other_x in range(2):
+            right_copies[unit][other_x].wait_recv()
+            for side in range(2):
+                source = (
+                    block_columns(unit, 2 * other_x + c) if side == 0 else far_right.at[unit, other_x]
+                )
+                copy = pltpu.make_async_copy(
+                    source,
+                    ybuf.at[slot, side, :, pl.ds(other_x * 256, 256)],
+                    load_sem.at[2 + slot, 2 * other_x + side],
+                )
+                copy.start()
+                started.append(copy)
+        return started
+
+    def multiply(unit):
+        xs, ys = left_slot[unit], unit % 2
+
+        def step(zi, carry):
+            columns = pl.ds(pl.multiple_of(zi * 256, 256), 256)
+            total = tn_dot(xbuf[xs, 0, :, columns], ybuf[ys, 0]) + tn_dot(
+                xbuf[xs, 1, :, columns], ybuf[ys, 1]
+            )
+            total = total.astype(jnp.bfloat16)
+            for yi in range(2):
+                for xi in range(2):
+                    block = total[yi * 128 : yi * 128 + 128, xi * 256 : xi * 256 + 256]
+                    part_a[unit, xi, yi, zi] = block[PARTS[0] : PARTS[1]]
+                    part_b[unit, yi, xi, zi] = block[PARTS[1] : PARTS[2]]
+                    part_c[unit, zi, xi, yi] = block[PARTS[2] : PARTS[3]]
+            return carry
+
+        lax.fori_loop(0, 4, step, 0)
+
+    is_end = (z == 0) | (z == 3)
+    is_mid = (z == 1) | (z == 2)
+
+    end_low = jnp.where(z == 0, 1, 0)
+    end_dir = jnp.where(z == 0, 0, 1)
+    end_next = (jnp.where(z == 0, 1, 2) * 2 + y, seq)
+    mid_dir = jnp.where(z == 1, 0, 1)
+    mid_low = jnp.where(z == 1, 1, 0)
+    mid_keep = jnp.where(z == 1, 2, 0)
+    mid_next = ((3 - z) * 2 + y, seq)
+    back_dir = 1 - mid_dir
+    back_low = jnp.where(z == 2, 2, 0)
+    back_keep = jnp.where(z == 2, 3, 0)
+    back_next = (jnp.where(z == 2, 3, 0) * 2 + y, seq)
+
+    def z_send(unit, which, pieces, recv, number):
+        ssem, rsem = send_sem.at[unit, which], recv_sem.at[unit, which]
+        if number == 0:
+            low, size, way, device = end_low, 3, end_dir, end_next
+        elif number == 1:
+            low, size, way, device = mid_keep, 2, mid_dir, mid_next
+        else:
+            low, size, way, device = back_keep, 1, back_dir, back_next
+        return remote(
+            pieces.at[pl.ds(low, size)], recv.at[way, pl.ds(low, size)],
+            ssem.at[2 + number // 2], rsem.at[2 + way], device,
+        )
+
+    def z_wait(unit, which, recv, direction, low, size):
+        view = recv.at[direction, pl.ds(low, size)]
+        pltpu.make_async_copy(view, view, recv_sem.at[unit, which, 2 + direction]).wait()
+
+    def z_round0(unit, which, pieces, recv):
+        @pl.when(is_end)
+        def _():
+            z_send(unit, which, pieces, recv, 0).start()
+
+    def z_round1(unit, which, pieces, recv):
+        @pl.when(is_mid)
+        def _():
+            z_wait(unit, which, recv, mid_dir, mid_low, 3)
+            keep = pl.ds(mid_keep, 2)
+            pieces[keep] = pieces[keep] + recv[mid_dir, keep]
+            z_send(unit, which, pieces, recv, 1).start()
+
+    def z_round2(unit, which, pieces, recv):
+        @pl.when(is_mid)
+        def _():
+            z_wait(unit, which, recv, back_dir, back_low, 2)
+            keep = pl.ds(back_keep, 1)
+            pieces[keep] = pieces[keep] + recv[back_dir, keep]
+            z_send(unit, which, pieces, recv, 2).start()
+
+    def z_final(unit, which, pieces, recv, finish):
+        @pl.when(is_end)
+        def _():
+            z_wait(unit, which, recv, 1 - end_dir, z, 1)
+            finish(
+                pieces[z].astype(jnp.float32) + recv[1 - end_dir, z].astype(jnp.float32)
+            )
+
+        @pl.when(is_mid)
+        def _():
+            finish(
+                pieces[z].astype(jnp.float32)
+                + recv[0, z].astype(jnp.float32)
+                + recv[1, z].astype(jnp.float32)
+            )
+
+    def send(unit, which, index, source, target, device):
+        copy = remote(
+            source, target, send_sem.at[unit, which, index], recv_sem.at[unit, which, index], device
+        )
+        copy.start()
+        sends.append(copy)
+        return copy
+
+    hops = {}
+
+    def put(unit, which, block):
+        _, _, _, _, _, offset, out, row = UNITS[unit]
+        outs[out][
+            row + PARTS[which] : row + PARTS[which + 1], offset : offset + 256
+        ] = block
+
+    def stage(unit, number):
+        a, b, cc = part_a.at[unit], part_b.at[unit], part_c.at[unit]
+        a_z, b_z = a.at[x, y], b.at[y, x]
+        rz_a, rz_b, rz_c = recv_az.at[unit], recv_bz.at[unit], recv_cz.at[unit]
+        if number == 0:
+            hops[unit, 0, 0] = send(unit, 0, 0, a.at[1 - x], recv_a1.at[unit], dev_x)
+            hops[unit, 1, 0] = send(unit, 1, 0, b.at[1 - y], recv_b1.at[unit], dev_y)
+            z_round0(unit, 2, cc, rz_c)
+        if number == 1:
+            hops[unit, 0, 0].wait_recv()
+            a[x] = a[x] + recv_a1[unit]
+            hops[unit, 0, 1] = send(unit, 0, 1, a.at[x, 1 - y], recv_a2.at[unit], dev_y)
+            hops[unit, 1, 0].wait_recv()
+            b[y] = b[y] + recv_b1[unit]
+            hops[unit, 1, 1] = send(unit, 1, 1, b.at[y, 1 - x], recv_b2.at[unit], dev_x)
+            z_round1(unit, 2, cc, rz_c)
+        if number == 2:
+            hops[unit, 0, 1].wait_recv()
+            a[x, y] = a[x, y] + recv_a2[unit]
+            z_round0(unit, 0, a_z, rz_a)
+            hops[unit, 1, 1].wait_recv()
+            b[y, x] = b[y, x] + recv_b2[unit]
+            z_round0(unit, 1, b_z, rz_b)
+            z_round2(unit, 2, cc, rz_c)
+        if number == 3:
+            z_round1(unit, 0, a_z, rz_a)
+            z_round1(unit, 1, b_z, rz_b)
+
+            def keep(value):
+                cc[z] = value.astype(jnp.bfloat16)
+
+            z_final(unit, 2, cc, rz_c, keep)
+            hops[unit, 2, 0] = send(unit, 2, 0, cc.at[z, 1 - x], recv_c1.at[unit], dev_x)
+        if number == 4:
+            z_round2(unit, 0, a_z, rz_a)
+            z_round2(unit, 1, b_z, rz_b)
+            hops[unit, 2, 0].wait_recv()
+            cc[z, x] = cc[z, x] + recv_c1[unit]
+            hops[unit, 2, 1] = send(unit, 2, 1, cc.at[z, x, 1 - y], recv_c2.at[unit], dev_y)
+        if number == 5:
+            z_final(unit, 0, a_z, rz_a, functools.partial(put, unit, 0))
+            z_final(unit, 1, b_z, rz_b, functools.partial(put, unit, 1))
+            hops[unit, 2, 1].wait_recv()
+            put(unit, 2, cc[z, x, y].astype(jnp.float32) + recv_c2[unit].astype(jnp.float32))
+
+    vec_hops = {}
+
+    def vec_stage(number):
+        if number == 0:
+            vec_sum[0] = vec_ref[...]
+        elif number <= 3:
+            vec_hops[number - 1].wait_recv()
+            vec_sum[number] = vec_sum[number - 1] + vec_recv[number - 1]
+        if number < 3:
+            copy = remote(
+                vec_sum.at[number], vec_recv.at[number], vec_send.at[number],
+                vec_rsem.at[number], (dev_c, dev_x, dev_y)[number],
+            )
+            copy.start()
+            sends.append(copy)
+            vec_hops[number] = copy
+        elif number == 3:
+            vec_z[z] = vec_sum[3]
+            for k in range(3):
+                copy = remote(
+                    vec_sum.at[3], vec_z.at[z], vec_send.at[3 + k], vec_rsem.at[3 + k], dev_z[k]
+                )
+                copy.start()
+                sends.append(copy)
+                vec_hops[3 + k] = copy
+        elif number == 4:
+            for k in range(3):
+                source = lax.rem(z + 3 - k, 4)
+                view = vec_z.at[source]
+                pltpu.make_async_copy(view, view, vec_rsem.at[3 + k]).wait()
+            vec_out[...] = vec_z[0] + vec_z[1] + vec_z[2] + vec_z[3]
+
+    loads = {0: load(0)}
+    for slot in range(count + 5 + LAG):
+        if slot + 1 < count:
+            loads[slot + 1] = load(slot + 1)
+        if slot < count:
+            for copy in loads[slot]:
+                copy.wait()
+            multiply(slot)
+            stage(slot, 0)
+        for number in range(1, 6):
+            unit = slot - number - LAG
+            if 0 <= unit < count:
+                stage(unit, number)
+        if slot < 5:
+            vec_stage(slot)
+
+    for copy in sends:
+        copy.wait_send()
+    for unit in range(count):
+        for which, (pieces, recv) in enumerate(
+            (
+                (part_a.at[unit, x, y], recv_az.at[unit]),
+                (part_b.at[unit, y, x], recv_bz.at[unit]),
+                (part_c.at[unit], recv_cz.at[unit]),
+            )
+        ):
+
+            @pl.when(is_end)
+            def _():
+                z_send(unit, which, pieces, recv, 0).wait_send()
+
+            @pl.when(is_mid)
+            def _():
+                z_send(unit, which, pieces, recv, 1).wait_send()
+                z_send(unit, which, pieces, recv, 2).wait_send()
+
+
+def reduce_weights(lefts, rights, vectors):
+    count = len(UNITS)
+    bf = jnp.bfloat16
+    hbm = pl.BlockSpec(memory_space=pl.ANY)
+    vmem = pl.BlockSpec(memory_space=pltpu.VMEM)
+    size = (PARTS[1], PARTS[2] - PARTS[1], PARTS[3] - PARTS[2])
+    f32 = jnp.float32
+    scratch = [
+        pltpu.VMEM((2, 2, TOK, 1024), bf),
+        pltpu.VMEM((2, 2, TOK, 512), bf),
+        pltpu.VMEM((count, 2, 2, 4, size[0], 256), bf),
+        pltpu.VMEM((count, 2, 2, 4, size[1], 256), bf),
+        pltpu.VMEM((count, 4, 2, 2, size[2], 256), bf),
+        pltpu.VMEM((count, 2, 4, size[0], 256), bf),
+        pltpu.VMEM((count, 4, size[0], 256), bf),
+        pltpu.VMEM((count, 2, 4, size[0], 256), bf),
+        pltpu.VMEM((count, 2, 4, size[1], 256), bf),
+        pltpu.VMEM((count, 4, size[1], 256), bf),
+        pltpu.VMEM((count, 2, 4, size[1], 256), bf),
+        pltpu.VMEM((count, 2, 4, 2, 2, size[2], 256), bf),
+        pltpu.VMEM((count, 2, size[2], 256), bf),
+        pltpu.VMEM((count, size[2], 256), bf),
+        pltpu.VMEM((4, 8, 1024), f32),
+        pltpu.VMEM((3, 8, 1024), f32),
+        pltpu.VMEM((4, 8, 1024), f32),
+        pltpu.SemaphoreType.DMA((4 + 2 * count,)),
+        pltpu.SemaphoreType.DMA((4 + 2 * count,)),
+        pltpu.SemaphoreType.DMA((4, 4)),
+        pltpu.SemaphoreType.DMA((count, 3, 4)),
+        pltpu.SemaphoreType.DMA((count, 3, 4)),
+        pltpu.SemaphoreType.DMA((6,)),
+        pltpu.SemaphoreType.DMA((6,)),
+    ]
+    shape = jax.ShapeDtypeStruct
+    return pl.pallas_call(
+        scatter_kernel,
+        out_shape=[
+            shape((128, 768), f32),
+            shape((128, 256), f32),
+            shape((128, 2048), f32),
+            shape((512, 256), f32),
+            shape((8, 1024), f32),
+        ]
+        + [shape(v.shape, bf) for v in lefts]
+        + [shape((count, 2, TOK, 256), bf)],
+        in_specs=[hbm] * 8 + [vmem],
+        out_specs=[vmem] * 5 + [hbm] * 5,
+        scratch_shapes=scratch,
+        compiler_params=pltpu.CompilerParams(
+            collective_id=1, has_side_effects=True, vmem_limit_bytes=62 * 2**20
+        ),
+        name="scatter_sums",
+    )(*lefts, *rights, vectors)[:5]
 
 
 def local(
@@ -214,16 +626,13 @@
     out_grad = cotangent.astype(jnp.float32)
     grad_scale_mlp = jnp.sum(out_grad * mlp_out, 0)
     mlp_grad = (out_grad * scale_mlp).astype(jnp.bfloat16)
-    grad_w_down = contract_rows(hidden_b, mlp_grad)
     hidden_grad = contract_back(mlp_grad, w_down)
     (gate_up_grad,) = gate_back(hidden_grad)
     gate_up_b = gate_up_grad.astype(jnp.bfloat16)
-    grad_w_gate_up = contract_rows(normed_two_b, gate_up_b)
     middle_part, grad_ln2_gain, grad_ln2_bias = norm_two_back(contract_back(gate_up_b, w_gate_up))
     middle_grad = out_grad + middle_part
     grad_scale_attn = jnp.sum(middle_grad * branch, 0)
     branch_grad = (middle_grad * scale_attn).astype(jnp.bfloat16)
-    grad_w_out = contract_rows(attended_t, branch_grad)
     attended_grad = contract_back(branch_grad, w_out).astype(jnp.bfloat16)
     grad_heads = lax.all_to_all(attended_grad, "seq", split_axis=1, concat_axis=0, tiled=True)
     query_grads, key_grads, value_grads = attention_backward(
@@ -257,7 +666,6 @@
         lax.all_to_all(value_back, "seq", split_axis=0, concat_axis=1, tiled=True),
     )
     projected_grad = jnp.concatenate([query_own, key_own, value_own], 1)
-    grad_w_qkv = contract_rows(normed_b, projected_grad)
     input_part, grad_ln1_gain, grad_ln1_bias = norm_back(contract_back(projected_grad, w_qkv))
     input_grad = middle_grad + input_part
     vector_grads = jnp.stack(
@@ -271,38 +679,25 @@
         ],
         0,
     )
-    vector_total = lax.psum(vector_grads, ("dp", "seq"))
     data_count = lax.axis_size("dp")
-    summed = (
-        lax.psum_scatter(
-            to_blocks(grad_w_qkv, data_count, seq_count),
-            ("dp", "seq"),
-            scatter_dimension=0,
-            tiled=True,
-        ),
-        lax.psum_scatter(
-            to_blocks(grad_w_out, data_count, seq_count),
-            ("dp", "seq"),
-            scatter_dimension=0,
-            tiled=True,
-        ),
-        lax.psum_scatter(
-            to_blocks(grad_w_gate_up, data_count, seq_count),
-            ("dp", "seq"),
-            scatter_dimension=0,
-            tiled=True,
-        ),
-        lax.psum_scatter(
-            to_blocks(grad_w_down, data_count, seq_count),
-            ("dp", "seq"),
-            scatter_dimension=0,
-            tiled=True,
-        ),
-    )
-    sum_qkv = summed[0][0]
-    sum_out = summed[1][0]
-    sum_gate_up = summed[2][0]
-    sum_down = summed[3][0]
+    lefts = (normed_b, attended_t, normed_two_b, hidden_b)
+    rights = (projected_grad, branch_grad, gate_up_b, mlp_grad)
+    if (data_count, seq_count, row_count) == (8, 4, TOK):
+        padded = jnp.concatenate([vector_grads, jnp.zeros((2, D), jnp.float32)], 0)
+        sum_qkv, sum_out, sum_gate_up, sum_down, vector_total = reduce_weights(
+            lefts, rights, padded
+        )
+    else:
+        vector_total = lax.psum(vector_grads, ("dp", "seq"))
+        sum_qkv, sum_out, sum_gate_up, sum_down = [
+            lax.psum_scatter(
+                to_blocks(contract_rows(left, right), data_count, seq_count),
+                ("dp", "seq"),
+                scatter_dimension=0,
+                tiled=True,
+            )[0]
+            for left, right in zip(lefts, rights)
+        ]
     return (
         out_frames,
         input_grad,

time: 1300 us -> 579 us (0.45)
  waiting for transfers between devices: 673 us -> 80.7 us
  Pallas kernels: 0 us -> 146 us
  local copies, waits for them, and re-layouts: 251 us -> 127 us
  blocking collectives: 95.1 us -> 0 us
  matrix products: 202 us -> 145 us
  between operations: 14.7 us -> 1.59 us
    reduce_scatter x4 -> x0, waiting for transfers between devices: 623 us -> none  [the longest x1 359 us: local(): lax.psum_scatter(to_blocks(grad_w_gate_up, data_count, seq_count), ('dp',...]
    pallas_call x0 -> x1, Pallas kernels: none -> 146 us  [reduce_weights(): pl.pallas_call(scatter_kernel, out_shape=[shape((128, 768), f32), shape((...]
    reshape x3 -> x0, local copies, waits for them, and re-layouts: 75.9 us -> none  [to_blocks(): matrix.reshape(data_count, row_total // data_count, seq_count, col_total...]
    transpose x3 -> x0, local copies, waits for them, and re-layouts: 58 us -> none  [to_blocks(): shaped.transpose(0, 2, 1, 3)]
    all_to_all x3 -> x0, blocking collectives: 53.8 us -> none  [the longest x1 18.6 us: local(): lax.all_to_all(rotated[:, :D], 'seq', split_axis=1, concat_axis=0, tiled=...]
    dot_general x4 -> x0, matrix products: 46.2 us -> none  [contract_rows(): lax.dot_general(left, right, (((0,), (0,)), ((), ())), preferred_element_...]
    psum x1 -> x0, blocking collectives: 41.3 us -> none  [local(): vector_total = lax.psum(vector_grads, ('dp', 'seq'))]
    all_to_all x0 -> x3, waiting for transfers between devices: none -> 40.6 us  [the longest x1 14.2 us: local(): lax.all_to_all(rotated[:, :D], 'seq', split_axis=1, concat_axis=0, tiled=...]
  transfers between devices with their start and end apart: 9 -> 8, of which waited for: 8 -> 7; matrix products, arithmetic and copies ran while one was open for 15% -> 6% of each run, Pallas kernels for 0% -> 0%
where the time goes in v1:
time: 579 us; the launch traced here: 572 us
  Pallas kernels  146 us (25%)
  matrix products  145 us (25%)
  local copies, waits for them, and re-layouts  127 us (22%)
  waiting for transfers between devices  80.7 us (14%)
  other arithmetic  34 us (6%)
  starting transfers between devices  31.7 us (5%)
    pallas_call x1, Pallas kernels, reduce_weights(): pl.pallas_call(scatter_kernel, out_shape=[shape((128, 768), f32), shape((...  146 us
    dynamic_update_slice x12, local copies, waits for them, and re-layouts, attention_forward(): lax.map(one_block, jnp.arange(queries.shape[0] // QBLK, dtype=jnp.int32))  46.5 us
    dot_general x4, matrix products, contract_back(): lax.dot_general(grads, weight, (((1,), (1,)), ((), ())), preferred_elemen...  45.3 us
    dot_general x8, matrix products, block_scores(): jnp.einsum('qhd,khd->hqk', q_block, k_block, preferred_element_type=jnp.f...  24.1 us
    unnamed x90, local copies, waits for them, and re-layouts  18.5 us
    dot_general x1, matrix products, local(): jnp.dot(normed_two_b, w_gate_up, preferred_element_type=jnp.float32)  15.7 us
    all_to_all x1, waiting for transfers between devices, local(): lax.all_to_all(rotated[:, :D], 'seq', split_axis=1, concat_axis=0, tiled=...  14.2 us
    all_to_all x1, waiting for transfers between devices, local(): lax.all_to_all(attended_grad, 'seq', split_axis=1, concat_axis=0, tiled=T...  13.4 us
  transfers between devices with their start and end apart: 8, of which 7 were waited for; matrix products, arithmetic and copies ran while one was open for 6% of the time, Pallas kernels for 0%

profile of v1, /device:TPU:0, one launch (start us, length us, event | category | flops | bytes accessed | tf_op | source)
XLA Modules:
  0.0 571.6 jit_solution(9600029370327050755)
XLA Ops:
  5.5 5.9 %fusion.75 = f32[512,3072]{1,0:T(8,128)S(1)} fusion(bf16[512,1024]{1,0:T(8,128)(2,1)S(1)} %fusion.59.left0, bf16[1024,3072]{1,0:T(8,128)(2,1)} %param.22), kind=kOutput, calls=%fused_computation.141 | convolution fusion | flops 3221225472 | bytes 13631488 | tf_op jit(solution)/shard_map/dot_general | solution.py:591
  11.4 2.7 copy-done.7
  15.3 4.2 all-to-all-start
  19.5 4.7 slice.85
  24.2 5.4 copy.83
  29.9 2.9 subtract_convert_fusion
  34.5 3.6 all-to-all-start.1
  38.4 14.2 %all-to-all-done.1 = bf16[512,4,256]{0,2,1:T(8,128)(2,1)S(1)} async-done(((bf16[512,4,256]{0,2,1:T(8,128)(2,1)}), bf16[512,4,256]{0,2,1:T(8,128)(2,1)S(1)}, u32[]{:S(2)}, u32[]{:S(2)}) %all-to-all-start.1) | async-done | bytes 1048608 | tf_op jit(solution)/shard_map/all_to_all | solution.py:598
  52.7 4.8 all-to-all-start.2
  65.7 6.3 %all-to-all-done.2 = bf16[512,4,256]{0,2,1:T(8,128)(2,1)} async-done(((bf16[512,4,256]{0,2,1:T(8,128)(2,1)}), bf16[512,4,256]{0,2,1:T(8,128)(2,1)}, u32[]{:S(2)}, u32[]{:S(2)}) %all-to-all-start.2) | async-done | bytes 1048608 | tf_op jit(solution)/shard_map/all_to_all | solution.py:599
  72.0 3.0 copy.85
  79.8 33.2 %while.28 = (s32[]{:T(128)}, bf16[4,512,4,64]{1,3,2,0:T(8,128)(2,1)S(1)}, f32[4,4,512,1]{2,1,3,0:T(4,128)S(1)}, f32[4,4,512,1]{2,1,3,0:T(4,128)S(1)}, s32[4]{0:T...) while((s32[]{:T(128)}, ...), condition=%wide.region_8.9_spmd, body=%wide.region_5.8_spmd.sunk | while | flops 353234944 | bytes 18568964 | solution.py:95
  85.2 2.8 fusion.117
  93.5 2.8 fusion.117
  101.8 2.8 fusion.117
  110.2 2.8 fusion.117
  116.3 3.7 all-to-all-start.3
  121.3 13.2 %all-to-all-done.3 = bf16[4,512,256]{2,1,0:T(8,128)(2,1)S(1)} async-done(((bf16[4,512,256]{2,1,0:T(8,128)(2,1)}), bf16[4,512,256]{2,1,0:T(8,128)(2,1)S(1)}, u32[]{:S(2)}, u32[]{:S(2)}) %all-to-all-start.3) | async-done | bytes 1048608 | tf_op jit(solution)/shard_map/all_to_all | solution.py:610
  136.4 2.6 fusion.72
  141.2 15.7 %fusion.76 = f32[512,8192]{1,0:T(8,128)} fusion(bf16[512,1024]{1,0:T(8,128)(2,1)S(1)} %add_convert_fusion.2.left2, bf16[1024,8192]{1,0:T(8,128)(2,1)} %param.27), kind=kOutput, calls=%fused_computation.142 | convolution fusion | flops 8589934592 | bytes 34603008 | tf_op jit(solution)/shard_map/dot_general | solution.py:621
  156.9 21.4 %fusion.65 = (f32[512,4096]{1,0:T(8,128)}, f32[512,4096]{1,0:T(8,128)}, bf16[512,4096]{1,0:T(8,128)(2,1)}) fusion(f32[512,8192]{1,0:T(8,128)} %fusion.76, bf16[512,1024]{1,0:T(8,128)(2,1)S(1)} %copy-done.14, bf16[4096,1024]{1,0:T(8,128)(2,1)} %param.28), kind=kOutput, calls=%fused_computation.107 | convolution fusion | flops 4324327424 | bytes 47185920 | tf_op jit(solution)/shard_map/dot_general | solution.py:63
  178.3 9.0 %add_convert_fusion.right2 = bf16[512,8192]{1,0:T(8,128)(2,1)} fusion(f32[512,4096]{1,0:T(8,128)} %get-tuple-element.232, f32[512,4096]{1,0:T(8,128)} %get-tuple-element.231), kind=kLoop, calls=%fused_computation.57 | loop fusion | flops 8388608 | bytes 25165824 | tf_op jit(solution)/shard_map/convert_element_type | solution.py:631
  187.4 15.3 %multiply_reduce_fusion.1 = (f32[1024]{0:T(1024)S(1)}, f32[512]{0:T(512)S(1)}, f32[1024]{0:T(1024)S(1)}, f32[512,1024]{1,0:T(8,128)S(1)}) fusion(f32[512,1024]{1,0:T(8,128)S(1)} %get-tuple-element.222, f32[512]{0:T(512)S(1)} %fusion.68, f32[512]{0:T(512)S(1)} %broadcast_multiply_fusion, f32[1024]{0:T(1024)S(1)} %copy-done.29, ...), kind=kOutput, calls=%fused_computation.88 | convolution fusion | flops 8594125824 | bytes 29378560 | tf_op jit(solution)/shard_map/dot_general | solution.py:63
  208.1 3.9 all-to-all-start.4
  213.1 13.4 %all-to-all-done.4 = bf16[512,4,256]{2,0,1:T(8,128)(2,1)S(1)} async-done(((bf16[512,4,256]{2,0,1:T(8,128)(2,1)}), bf16[512,4,256]{2,0,1:T(8,128)(2,1)S(1)}, u32[]{:S(2)}, u32[]{:S(2)}) %all-to-all-start.4) | async-done | bytes 1048608 | tf_op jit(solution)/shard_map/all_to_all | solution.py:637
  230.8 102.6 %while.29 = (s32[]{:T(128)}, f32[2176,4,64]{0,2,1:T(8,128)S(1)}, f32[2176,4,64]{0,2,1:T(8,128)}, f32[4,512,4,64]{1,0,3,2:T(4,128)}, s32[4]{0:T(128)S(1)}, /*inde...) while((s32[]{:T(128)}, f32[2176,4,64]{0,2,1:T(8,128)S(1)}, ...), condition=%wide.region_15.16_spmd, body=%wide.region_13.15_spmd.sunk | while | flops 854554624 | bytes 47331124 | solution.py:142
  234.4 3.7 multiply_reduce_fusion.6
  240.2 2.7 fusion.129
  245.4 11.1 %dynamic_update_slice.34 = f32[4,512,4,64]{1,0,3,2:T(4,128)} dynamic-update-slice(f32[4,512,4,64]{1,0,3,2:T(4,128)} %get-tuple-element.483, f32[1,512,4,64]{1,0,3,2:T(1,128)S(1)} %copy.126, s32[]{:T(128)S(6)} %copy.149, s32[]{:T(128)} %constant.61.clone.1..sunk.1, s32[]{:T(128)} %constant.61.clone.1..sunk.1, s32[]{:T(128)} %constant.61.clone.1..sunk.1) | dynamic-update-slice | bytes 1048580 | tf_op jit(solution)/shard_map/while/body/jit(dynamic_update_index_in_dim)/dynamic_update_slice | solution.py:95
  260.0 3.7 multiply_reduce_fusion.6
  265.9 2.7 fusion.129
  271.0 11.1 %dynamic_update_slice.34 = f32[4,512,4,64]{1,0,3,2:T(4,128)} dynamic-update-slice(f32[4,512,4,64]{1,0,3,2:T(4,128)} %get-tuple-element.483, f32[1,512,4,64]{1,0,3,2:T(1,128)S(1)} %copy.126, s32[]{:T(128)S(6)} %copy.149, s32[]{:T(128)} %constant.61.clone.1..sunk.1, s32[]{:T(128)} %constant.61.clone.1..sunk.1, s32[]{:T(128)} %constant.61.clone.1..sunk.1) | dynamic-update-slice | bytes 1048580 | tf_op jit(solution)/shard_map/while/body/jit(dynamic_update_index_in_dim)/dynamic_update_slice | solution.py:95
  285.7 3.7 multiply_reduce_fusion.6
  291.5 2.7 fusion.129
  296.7 11.1 %dynamic_update_slice.34 = f32[4,512,4,64]{1,0,3,2:T(4,128)} dynamic-update-slice(f32[4,512,4,64]{1,0,3,2:T(4,128)} %get-tuple-element.483, f32[1,512,4,64]{1,0,3,2:T(1,128)S(1)} %copy.126, s32[]{:T(128)S(6)} %copy.149, s32[]{:T(128)} %constant.61.clone.1..sunk.1, s32[]{:T(128)} %constant.61.clone.1..sunk.1, s32[]{:T(128)} %constant.61.clone.1..sunk.1) | dynamic-update-slice | bytes 1048580 | tf_op jit(solution)/shard_map/while/body/jit(dynamic_update_index_in_dim)/dynamic_update_slice | solution.py:95
  311.4 3.7 multiply_reduce_fusion.6
  317.2 2.7 fusion.129
  322.4 11.1 %dynamic_update_slice.34 = f32[4,512,4,64]{1,0,3,2:T(4,128)} dynamic-update-slice(f32[4,512,4,64]{1,0,3,2:T(4,128)} %get-tuple-element.483, f32[1,512,4,64]{1,0,3,2:T(1,128)S(1)} %copy.126, s32[]{:T(128)S(6)} %copy.149, s32[]{:T(128)} %constant.61.clone.1..sunk.1, s32[]{:T(128)} %constant.61.clone.1..sunk.1, s32[]{:T(128)} %constant.61.clone.1..sunk.1) | dynamic-update-slice | bytes 1048580 | tf_op jit(solution)/shard_map/while/body/jit(dynamic_update_index_in_dim)/dynamic_update_slice | solution.py:95
  333.4 3.7 reshape.402
  342.1 3.5 all-to-all-start.5
  348.0 12.0 %all-to-all-done.5 = bf16[4,512,256]{2,1,0:T(8,128)(2,1)S(1)} async-done(((bf16[4,512,256]{2,1,0:T(8,128)(2,1)}), bf16[4,512,256]{2,1,0:T(8,128)(2,1)S(1)}, u32[]{:S(2)}, u32[]{:S(2)}) %all-to-all-start.5) | async-done | bytes 1048608 | tf_op jit(solution)/shard_map/all_to_all | solution.py:664
  360.0 3.5 all-to-all-start.6
  369.5 8.4 %all-to-all-done.6 = bf16[4,512,256]{2,1,0:T(8,128)(2,1)S(1)} async-done(((bf16[4,512,256]{2,1,0:T(8,128)(2,1)}), bf16[4,512,256]{2,1,0:T(8,128)(2,1)S(1)}, u32[]{:S(2)}, u32[]{:S(2)}) %all-to-all-start.6) | async-done | bytes 1048608 | tf_op jit(solution)/shard_map/all_to_all | solution.py:665
  378.0 4.4 all-to-all-start.7
  383.7 13.2 %all-to-all-done.7 = bf16[4,512,256]{2,1,0:T(8,128)(2,1)} async-done(((bf16[4,512,256]{2,1,0:T(8,128)(2,1)}), bf16[4,512,256]{2,1,0:T(8,128)(2,1)}, u32[]{:S(2)}, u32[]{:S(2)}) %all-to-all-start.7) | async-done | bytes 1048608 | tf_op jit(solution)/shard_map/all_to_all | solution.py:666
  399.7 7.3 %fusion.70 = (f32[1024]{0:T(1024)S(1)}, f32[512]{0:T(512)S(1)}, f32[512,1024]{1,0:T(8,128)S(1)}) fusion(f32[1024]{0:T(1024)S(1)} %copy-done.28, f32[512]{0:T(512)S(1)} %copy-done.22, bf16[512,1024]{1,0:T(8,128)(2,1)S(1)} %copy-done.3, bf16[512,3072]{1,0:T(8,128)(2,1)S(1)} %constant_dynamic-update-slice_fusion.right0, bf16[1024,3072]{1,0:T(8,128)(2,1)} %param.22), kind=kOutput, calls=%fused_computation.136 | convolution fusion | flops 3224369664 | bytes 12595200 | tf_op jit(solution)/shard_map/dot_general | solution.py:63
  408.9 7.6 %fusion.64 = (f32[1024]{0:T(1024)S(1)}, f32[1024]{0:T(1024)S(1)}, f32[512,1024]{1,0:T(8,128)}, bf16[512,1024]{1,0:T(8,128)(2,1)}) fusion(bf16[512,1024]{1,0:T(8,128)(2,1)S(1)} %copy-done.12, f32[512,1024]{1,0:T(8,128)} %get-tuple-element.256, f32[512,1024]{1,0:T(8,128)S(1)} %copy-done.5, f32[512]{0:T(512)S(1)} %negate_multiply_fusion.1, ...), kind=kOutput, calls=%fused_computation.84 | convolution fusion | flops 4304926720 | bytes 26241024 | tf_op jit(solution)/shard_map/dot_general | solution.py:624
  417.2 146.1 %scatter_sums.1 = (f32[128,768]{1,0:T(8,128)}, f32[128,256]{1,0:T(8,128)}, f32[128,2048]{1,0:T(8,128)}, f32[512,256]{1,0:T(8,128)}, f32[8,1024]{1,0:T(8,128)}, /...) custom-call(bf16[512,1024]{1,0:T(8,128)(2,1)} %copy-done.13, ...), custom_call_target="tpu_custom_call" | custom-call | tf_op jit(solution)/shard_map/scatter_sums/pallas_call | solution.py:547
  (228 shorter events, 117.5 us)
Async XLA Ops:
  0.6 4.4 copy-start.2
  0.7 4.4 copy-start.30
  0.7 4.4 copy-start.27
  2.2 2.2 copy-start.21
  5.5 5.9 %copy-start.13 = (bf16[512,1024]{1,0:T(8,128)(2,1)}, bf16[512,1024]{1,0:T(8,128)(2,1)S(1)}, u32[]{:S(2)}) copy-start(bf16[512,1024]{1,0:T(8,128)(2,1)S(1)} %fusion.59.left0) | copy-start | bytes 3145732
  11.4 2.7 copy-start.7
  15.3 19.3 %all-to-all-start = ((bf16[512,4,256]{2,0,1:T(8,128)(2,1)}), bf16[512,4,256]{2,0,1:T(8,128)(2,1)S(1)}, u32[]{:S(2)}, u32[]{:S(2)}) async-start(bf16[512,4,256]{2,0,1:T(8,128)(2,1)} %bitcast.108), calls=%async_computation | async-start | bytes 2097152 | tf_op jit(solution)/shard_map/all_to_all | solution.py:600
  24.2 5.4 copy-start.35
  34.5 3.7 copy-start.39
  34.5 18.1 %all-to-all-start.1 = ((bf16[512,4,256]{0,2,1:T(8,128)(2,1)}), bf16[512,4,256]{0,2,1:T(8,128)(2,1)S(1)}, u32[]{:S(2)}, u32[]{:S(2)}) async-start(bf16[512,4,256]{0,2,1:T(8,128)(2,1)} %bitcast.144), calls=%async_computation.1 | async-start | bytes 2097152 | tf_op jit(solution)/shard_map/all_to_all | solution.py:598
  52.7 19.3 %all-to-all-start.2 = ((bf16[512,4,256]{0,2,1:T(8,128)(2,1)}), bf16[512,4,256]{0,2,1:T(8,128)(2,1)}, u32[]{:S(2)}, u32[]{:S(2)}) async-start(bf16[512,4,256]{0,2,1:T(8,128)(2,1)} %bitcast.143), calls=%async_computation.2 | async-start | bytes 2097152 | tf_op jit(solution)/shard_map/all_to_all | solution.py:599
  78.2 1.5 copy-start.18
  113.0 1.0 copy-start.19
  114.0 6.1 %copy-start.10 = (bf16[512,1024]{1,0:T(8,128)(2,1)S(1)}, bf16[512,1024]{1,0:T(8,128)(2,1)}, u32[]{:S(2)}) copy-start(bf16[512,1024]{1,0:T(8,128)(2,1)} %param.18) | copy-start | bytes 3145732
  114.0 6.1 %copy-start.33 = (f32[1024]{0:T(1024)S(1)}, f32[1024]{0:T(1024)}, u32[]{:S(2)}) copy-start(f32[1024]{0:T(1024)} %param.29) | copy-start | bytes 12292
  116.3 18.1 %all-to-all-start.3 = ((bf16[4,512,256]{2,1,0:T(8,128)(2,1)}), bf16[4,512,256]{2,1,0:T(8,128)(2,1)S(1)}, u32[]{:S(2)}, u32[]{:S(2)}) async-start(bf16[4,512,256]{2,1,0:T(8,128)(2,1)} %copy.86), calls=%async_computation.3 | async-start | bytes 2097152 | tf_op jit(solution)/shard_map/all_to_all | solution.py:610
  120.1 14.5 %copy-start.32 = (f32[1024]{0:T(1024)S(1)}, f32[1024]{0:T(1024)}, u32[]{:S(2)}) copy-start(f32[1024]{0:T(1024)} %param.24) | copy-start | bytes 12292
  134.5 2.0 copy-start.37
  134.6 4.5 copy-start.15
  139.1 63.6 %copy-start = (f32[512,1024]{1,0:T(8,128)}, f32[512,1024]{1,0:T(8,128)S(1)}, u32[]{:S(2)}) copy-start(f32[512,1024]{1,0:T(8,128)S(1)} %get-tuple-element.222) | copy-start | bytes 6291460
  139.1 0.7 copy-start.29
  139.1 0.7 copy-start.31
  140.2 1.0 copy-start.16
  141.2 15.7 %copy-start.14 = (bf16[512,1024]{1,0:T(8,128)(2,1)S(1)}, bf16[512,1024]{1,0:T(8,128)(2,1)}, u32[]{:S(2)}) copy-start(bf16[512,1024]{1,0:T(8,128)(2,1)} %fusion.63.right3) | copy-start | bytes 3145732
  202.7 1.2 copy-start.11
  203.4 1.4 copy-start.4
  203.9 1.8 copy-start.38
  205.7 1.3 copy-start.9
  207.1 5.0 copy-start.36
  208.1 18.3 %all-to-all-start.4 = ((bf16[512,4,256]{2,0,1:T(8,128)(2,1)}), bf16[512,4,256]{2,0,1:T(8,128)(2,1)S(1)}, u32[]{:S(2)}, u32[]{:S(2)}) async-start(bf16[512,4,256]{2,0,1:T(8,128)(2,1)} %bitcast.107), calls=%async_computation.4 | async-start | bytes 2097152 | tf_op jit(solution)/shard_map/all_to_all | solution.py:637
  342.1 18.0 %all-to-all-start.5 = ((bf16[4,512,256]{2,1,0:T(8,128)(2,1)}), bf16[4,512,256]{2,1,0:T(8,128)(2,1)S(1)}, u32[]{:S(2)}, u32[]{:S(2)}) async-start(bf16[4,512,256]{2,1,0:T(8,128)(2,1)} %copy.91), calls=%async_computation.5 | async-start | bytes 2097152 | tf_op jit(solution)/shard_map/all_to_all | solution.py:664
  360.0 18.0 %all-to-all-start.6 = ((bf16[4,512,256]{2,1,0:T(8,128)(2,1)}), bf16[4,512,256]{2,1,0:T(8,128)(2,1)S(1)}, u32[]{:S(2)}, u32[]{:S(2)}) async-start(bf16[4,512,256]{2,1,0:T(8,128)(2,1)} %copy.93), calls=%async_computation.6 | async-start | bytes 2097152 | tf_op jit(solution)/shard_map/all_to_all | solution.py:665
  378.0 18.9 %all-to-all-start.7 = ((bf16[4,512,256]{2,1,0:T(8,128)(2,1)}), bf16[4,512,256]{2,1,0:T(8,128)(2,1)}, u32[]{:S(2)}, u32[]{:S(2)}) async-start(bf16[4,512,256]{2,1,0:T(8,128)(2,1)} %copy.95), calls=%async_computation.7 | async-start | bytes 2097152 | tf_op jit(solution)/shard_map/all_to_all | solution.py:666
  396.9 1.5 copy-start.17
  398.4 1.2 copy-start.3
  398.4 1.2 copy-start.22
  398.5 1.2 copy-start.28
  398.5 9.6 %slice-start = ((s8[8388608]{0:T(1024)(128)(4,1)}), s8[4194304]{0:T(1024)(128)(4,1)S(1)}, s32[]{:S(2)}) async-start(s8[8388608]{0:T(1024)(128)(4,1)} %bitcast.161), calls=%async_computation.8 | async-start | bytes 8388608
  399.7 7.4 %copy-start.6 = (bf16[512,3072]{1,0:T(8,128)(2,1)}, bf16[512,3072]{1,0:T(8,128)(2,1)S(1)}, u32[]{:S(2)}) copy-start(bf16[512,3072]{1,0:T(8,128)(2,1)S(1)} %constant_dynamic-update-slice_fusion.right0) | copy-start | bytes 9437188
  399.7 7.4 %copy-start.24 = (f32[512]{0:T(512)S(1)}, f32[512]{0:T(512)}, u32[]{:S(2)}) copy-start(f32[512]{0:T(512)} %copy-done.23) | copy-start | bytes 6148
  399.7 7.5 %copy-start.26 = (f32[512]{0:T(512)S(1)}, f32[512]{0:T(512)}, u32[]{:S(2)}) copy-start(f32[512]{0:T(512)} %copy-done.25) | copy-start | bytes 6148
  399.7 8.4 %copy-start.5 = (f32[512,1024]{1,0:T(8,128)S(1)}, f32[512,1024]{1,0:T(8,128)}, u32[]{:S(2)}) copy-start(f32[512,1024]{1,0:T(8,128)} %copy-done.4) | copy-start | bytes 6291460
  399.7 8.4 %copy-start.8 = (bf16[512,4096]{1,0:T(8,128)(2,1)S(1)}, bf16[512,4096]{1,0:T(8,128)(2,1)}, u32[]{:S(2)}) copy-start(bf16[512,4096]{1,0:T(8,128)(2,1)} %get-tuple-element.233.left3) | copy-start | bytes 12582916
  399.7 8.4 %slice-start.1 = ((s8[8388608]{0:T(1024)(128)(4,1)}), s8[4194304]{0:T(1024)(128)(4,1)S(1)}, s32[]{:S(2)}) async-start(s8[8388608]{0:T(1024)(128)(4,1)} %bitcast.161), calls=%async_computation.9 | async-start | bytes 8388608
  407.1 1.6 copy-start.1
  407.1 1.8 copy-start.12
  407.1 1.8 copy-start.34
  563.3 7.2 %copy-start.20 = (f32[512,256]{1,0:T(8,128)S(1)}, f32[512,256]{1,0:T(8,128)}, u32[]{:S(2)}) copy-start(f32[512,256]{1,0:T(8,128)} %get-tuple-element.538) | copy-start | bytes 1572868
  (2 other events, 1.2 us)
